TPU v7x, 512 devices: a whole 4x8x8 slice. The times are simulated.
512 devices in a mesh: corpus: 256 (over z_lo, y, x, core), feat: 2 (over z_hi).
Axes of the slice: x: 4, y: 8, z: 8 (z_hi: 2, z_lo: 4; z = z_hi * 4 + z_lo), core: 2. Of those that a mesh axis runs over, the one named last changes fastest.
Arguments:
- fresh_embed: bfloat16 [65536, 1024], P('corpus', 'feat'), may hold values from -64 to 64
- replay_embed: bfloat16 [524288, 1024], P('corpus', 'feat'), may hold values from -64 to 64
Outputs:
- fresh_lse: float32 [65536], P('corpus')
- replay_lse: float32 [524288], P(('corpus', 'feat'))
All inputs are finite; a program needn't handle non-finite values.
Results may differ from a plain program's by a relative error of at most 0.0003.
Values may be sent and summed in bfloat16 or wider, within the bound.
A program may use at most 64 MiB of HBM per device.

v0:
```python
import math

import jax
import jax.numpy as jnp
from jax import lax
from jax.sharding import PartitionSpec as P

WINDOW = 8


NEG_FLOOR = -1e30


def shifted(value, axis, steps):
    count = lax.axis_size(axis)
    pairs = [(source, (source + steps) % count) for source in range(count)]
    return lax.ppermute(value, axis, pairs)


def merged(value, axis, join):
    pieces = jax.tree.map(lambda part: lax.all_gather(part, axis), value)
    head = jax.tree.map(lambda part: part[0], pieces)
    tail = jax.tree.map(lambda part: part[1:], pieces)
    so_far, _ = lax.scan(lambda so_far, share: (join(so_far, share), None), head, tail)
    return so_far


def fold_tile(visitors, slab_local, visit_max, visit_total, column_max, column_total, score_scale):
    scores = (
        lax.dot_general(
            visitors, slab_local, (((1,), (1,)), ((), ())), preferred_element_type=jnp.float32
        )
        * score_scale
    )
    next_row = jnp.maximum(visit_max, jnp.max(scores, axis=1))
    visit_total = visit_total * jnp.exp(visit_max - next_row) + jnp.sum(
        jnp.exp(scores - next_row[:, None]), axis=1
    )
    next_column = jnp.maximum(column_max, jnp.max(scores, axis=0))
    column_total = column_total * jnp.exp(column_max - next_column) + jnp.sum(
        jnp.exp(scores - next_column[None, :]), axis=0
    )
    return (next_row, visit_total, next_column, column_total)


def merge_parts(one_part, two_part):
    joined = jnp.maximum(one_part[0], two_part[0])
    return (
        joined,
        one_part[1] * jnp.exp(one_part[0] - joined) + two_part[1] * jnp.exp(two_part[0] - joined),
    )


def per_device(fresh_embed, replay_embed):
    full_width = fresh_embed.shape[1] * lax.axis_size("feat")
    score_scale = 0.25 / math.sqrt(full_width)
    half_rows = replay_embed.shape[0] // lax.axis_size("feat")
    visitors, whole_slab = (
        lax.all_gather(fresh_embed, "feat", axis=1, tiled=True),
        lax.all_gather(replay_embed, "feat", axis=1, tiled=True),
    )
    slab_local = lax.dynamic_slice_in_dim(
        whole_slab, lax.axis_index("feat") * half_rows, half_rows, 0
    )
    block_rows = visitors.shape[0]
    local_rows = slab_local.shape[0]
    column_max = jnp.full((local_rows,), NEG_FLOOR, jnp.float32)
    column_total = jnp.zeros((local_rows,), jnp.float32)
    visit_max = jnp.full((block_rows,), NEG_FLOOR, jnp.float32)
    visit_total = jnp.zeros((block_rows,), jnp.float32)
    reach = WINDOW // 2
    moving = shifted(visitors, "corpus", -reach)

    def travel(step_index, carried):
        moving, row_max, row_total, col_max, col_total = carried
        row_max, row_total, col_max, col_total = fold_tile(
            moving, slab_local, row_max, row_total, col_max, col_total, score_scale
        )
        moving = shifted(moving, "corpus", 1)
        row_max, row_total = shifted((row_max, row_total), "corpus", 1)
        return (moving, row_max, row_total, col_max, col_total)

    finished = lax.fori_loop(
        0, WINDOW, travel, (moving, visit_max, visit_total, column_max, column_total)
    )
    visit_max, visit_total = shifted((finished[1], finished[2]), "corpus", -reach)
    column_max, column_total = (finished[3], finished[4])
    shared_max, shared_total = (visit_max, visit_total)
    shared_max, shared_total = merged((shared_max, shared_total), "feat", merge_parts)
    return (shared_max + jnp.log(shared_total), column_max + jnp.log(column_total))


def solution(mesh):
    placed = (P("corpus", "feat"), P("corpus", "feat"))
    return jax.shard_map(
        per_device,
        mesh=mesh,
        in_specs=placed,
        out_specs=(P("corpus"), P(("corpus", "feat"))),
        check_vma=False,
    )
```

profile of v0, /device:TPU:1, one launch (start us, length us, event | category | flops | bytes accessed | tf_op | source)
XLA Modules:
  0.0 303.7 jit_solution(10451076552611884260)
XLA Ops:
  8.1 15.6 %all_gather.18 = bf16[256,1024]{1,0:T(8,128)(2,1)S(1)} all-gather(bf16[256,512]{1,0:T(8,128)(2,1)S(1)} %copy-done), channel_id=1, replica_groups=mesh['corpus'=256,'feat'=2] {'feat'}, dimensions={1}, use_global_device_ids=true | all-gather | bytes 786432 | tf_op jit(solution)/shard_map/all_gather | solution.py:59
  23.7 12.8 %collective-permute-start.3 = (bf16[256,1024]{1,0:T(8,128)(2,1)S(1)}, bf16[256,1024]{1,0:T(8,128)(2,1)S(1)}, u32[]{:S(2)}, u32[]{:S(2)}) collective-permute-start(bf16[256,1024]{1,0:T(8,128)(2,1)S(1)} %all_gather.18), channel_id=1, source_target_pairs={{0,504},{2,506},{4,508},{6,510},{8,0},{10,2},{12,4},{14,6},{16,8},... | collective-permute-start | bytes 1572872 | tf_op jit(solution)/shard_map/ppermute | solution.py:17
  36.6 93.9 %all-gather.6.cloned.1.call-done = bf16[2048,1024]{1,0:T(8,128)(2,1)} async-done(((bf16[2048,512]{1,0:T(8,128)(2,1)}), bf16[2048,1024]{1,0:T(8,128)(2,1)}) %all-gather.6.cloned.1.call-update) | async-done | bytes 4194320 | tf_op jit(solution)/shard_map/all_gather | solution.py:60
  130.5 3.1 %constant_dynamic-slice_fusion = bf16[1024,1024]{1,0:T(8,128)(2,1)} fusion(bf16[2048,1024]{1,0:T(8,128)(2,1)} %all-gather.6.cloned.1.call-done, s32[]{:T(128)S(6)} %select_n.3), kind=kLoop, calls=%fused_computation.12 | loop fusion | bytes 4194308 | tf_op jit(solution)/shard_map/dynamic_slice | solution.py:62
  133.6 135.2 %while.6 = (s32[]{:T(128)}, bf16[256,1024]{1,0:T(8,128)(2,1)S(1)}, f32[256]{0:T(256)S(1)}, f32[256]{0:T(256)S(1)}, f32[1024]{0:T(1024)S(1)}, /*index=5*/f32[1024...) while((s32[]{:T(128)}, bf16[256,1024]{1,0:T(8,128)(2,1)S(1)}, f32[256]{0:T(256)S(1)}, ...), condition=%wide.region_5.0_spmd.clone, body=%wide.region_0.0_spmd.clone.sunk | while | flops 538711552 | bytes 7939296 | solution.py:83
  133.6 3.7 %collective-permute-start = (bf16[256,1024]{1,0:T(8,128)(2,1)S(1)}, bf16[256,1024]{1,0:T(8,128)(2,1)S(1)}, u32[]{:S(2)}, u32[]{:S(2)}) collective-permute-start(bf16[256,1024]{1,0:T(8,128)(2,1)S(1)} %copy.11), channel_id=1, source_target_pairs={{0,2},{2,4},{4,6},{6,8},{8,10},{10,12},{12,14},{14,16},{16,18},{18... | collective-permute-start | bytes 1572872 | tf_op jit(solution)/shard_map/while/body/eval_jaxpr/ppermute | solution.py:17
  137.3 2.4 fusion.14
  142.1 3.5 %collective-permute-start.2 = (f32[256]{0:T(256)S(1)}, f32[256]{0:T(256)S(1)}, u32[]{:S(2)}, u32[]{:S(2)}) collective-permute-start(f32[256]{0:T(256)S(1)} %multiply_add_fusion.2), channel_id=1, source_target_pairs={{0,2},{2,4},{4,6},{6,8},{8,10},{10,12},{12,14},{14,16},{16,18},{18... | collective-permute-start | bytes 3080 | tf_op jit(solution)/shard_map/while/body/eval_jaxpr/ppermute | solution.py:17
  146.4 4.2 %collective-permute-start = (bf16[256,1024]{1,0:T(8,128)(2,1)S(1)}, bf16[256,1024]{1,0:T(8,128)(2,1)S(1)}, u32[]{:S(2)}, u32[]{:S(2)}) collective-permute-start(bf16[256,1024]{1,0:T(8,128)(2,1)S(1)} %copy.11), channel_id=1, source_target_pairs={{0,2},{2,4},{4,6},{6,8},{8,10},{10,12},{12,14},{14,16},{16,18},{18... | collective-permute-start | bytes 1572872 | tf_op jit(solution)/shard_map/while/body/eval_jaxpr/ppermute | solution.py:17
  150.5 2.4 fusion.14
  155.3 3.2 %collective-permute-start.2 = (f32[256]{0:T(256)S(1)}, f32[256]{0:T(256)S(1)}, u32[]{:S(2)}, u32[]{:S(2)}) collective-permute-start(f32[256]{0:T(256)S(1)} %multiply_add_fusion.2), channel_id=1, source_target_pairs={{0,2},{2,4},{4,6},{6,8},{8,10},{10,12},{12,14},{14,16},{16,18},{18... | collective-permute-start | bytes 3080 | tf_op jit(solution)/shard_map/while/body/eval_jaxpr/ppermute | solution.py:17
  160.5 2.4 collective-permute-done.2
  164.8 2.4 fusion.14
  171.8 6.4 %collective-permute-done.1 = f32[256]{0:T(256)S(1)} collective-permute-done((f32[256]{0:T(256)S(1)}, f32[256]{0:T(256)S(1)}, u32[]{:S(2)}, u32[]{:S(2)}) %collective-permute-start.1) | collective-permute-done | bytes 1056 | tf_op jit(solution)/shard_map/while/body/eval_jaxpr/ppermute | solution.py:17
  178.1 2.4 collective-permute-done.2
  182.5 2.4 fusion.14
  189.2 6.6 %collective-permute-done.1 = f32[256]{0:T(256)S(1)} collective-permute-done((f32[256]{0:T(256)S(1)}, f32[256]{0:T(256)S(1)}, u32[]{:S(2)}, u32[]{:S(2)}) %collective-permute-start.1) | collective-permute-done | bytes 1056 | tf_op jit(solution)/shard_map/while/body/eval_jaxpr/ppermute | solution.py:17
  195.8 2.4 collective-permute-done.2
  200.1 2.4 fusion.14
  206.9 6.6 %collective-permute-done.1 = f32[256]{0:T(256)S(1)} collective-permute-done((f32[256]{0:T(256)S(1)}, f32[256]{0:T(256)S(1)}, u32[]{:S(2)}, u32[]{:S(2)}) %collective-permute-start.1) | collective-permute-done | bytes 1056 | tf_op jit(solution)/shard_map/while/body/eval_jaxpr/ppermute | solution.py:17
  213.5 2.4 collective-permute-done.2
  217.8 2.4 fusion.14
  224.5 6.6 %collective-permute-done.1 = f32[256]{0:T(256)S(1)} collective-permute-done((f32[256]{0:T(256)S(1)}, f32[256]{0:T(256)S(1)}, u32[]{:S(2)}, u32[]{:S(2)}) %collective-permute-start.1) | collective-permute-done | bytes 1056 | tf_op jit(solution)/shard_map/while/body/eval_jaxpr/ppermute | solution.py:17
  231.1 2.4 collective-permute-done.2
  235.4 2.4 fusion.14
  242.2 6.6 %collective-permute-done.1 = f32[256]{0:T(256)S(1)} collective-permute-done((f32[256]{0:T(256)S(1)}, f32[256]{0:T(256)S(1)}, u32[]{:S(2)}, u32[]{:S(2)}) %collective-permute-start.1) | collective-permute-done | bytes 1056 | tf_op jit(solution)/shard_map/while/body/eval_jaxpr/ppermute | solution.py:17
  248.8 2.4 collective-permute-done.2
  253.1 2.4 fusion.14
  259.8 6.6 %collective-permute-done.1 = f32[256]{0:T(256)S(1)} collective-permute-done((f32[256]{0:T(256)S(1)}, f32[256]{0:T(256)S(1)}, u32[]{:S(2)}, u32[]{:S(2)}) %collective-permute-start.1) | collective-permute-done | bytes 1056 | tf_op jit(solution)/shard_map/while/body/eval_jaxpr/ppermute | solution.py:17
  268.8 10.9 %collective-permute-start.4 = (f32[256]{0:T(256)S(1)}, f32[256]{0:T(256)S(1)}, u32[]{:S(2)}, u32[]{:S(2)}) collective-permute-start(f32[256]{0:T(256)S(1)} %get-tuple-element.57), channel_id=1, source_target_pairs={{0,504},{2,506},{4,508},{6,510},{8,0},{10,2},{12,4},{14,6},{16,8},... | collective-permute-start | bytes 3080 | tf_op jit(solution)/shard_map/ppermute | solution.py:17
  282.2 7.0 %all-gather.2 = f32[2,1,256]{2,1,0:T(1,128)S(1)} all-gather(f32[1,1,256]{2,1,0:T(1,128)S(1)} %bitcast.17), channel_id=2, replica_groups=mesh['corpus'=256,'feat'=2] {'feat'}, dimensions={0}, use_global_device_ids=true | all-gather | bytes 3072 | tf_op jit(solution)/shard_map/all_gather | solution.py:21
  289.2 7.0 %all-gather.3 = f32[2,1,256]{2,1,0:T(1,128)S(1)} all-gather(f32[1,1,256]{2,1,0:T(1,128)S(1)} %bitcast.16), channel_id=3, replica_groups=mesh['corpus'=256,'feat'=2] {'feat'}, dimensions={0}, use_global_device_ids=true | all-gather | bytes 3072 | tf_op jit(solution)/shard_map/all_gather | solution.py:21
  (112 shorter events, 51.4 us)
Async XLA Ops:
  7.2 1.0 copy-start
  7.2 123.3 %all-gather.6.cloned.1.call-start = ((), (), s32[]{:S(2)}) async-start(), calls=%async_computation | async-start | bytes 6291456 | tf_op jit(solution)/shard_map/all_gather | solution.py:60
  23.7 109.8 %collective-permute-start.3 = (bf16[256,1024]{1,0:T(8,128)(2,1)S(1)}, bf16[256,1024]{1,0:T(8,128)(2,1)S(1)}, u32[]{:S(2)}, u32[]{:S(2)}) collective-permute-start(bf16[256,1024]{1,0:T(8,128)(2,1)S(1)} %all_gather.18), channel_id=1, source_target_pairs={{0,504},{2,506},{4,508},{6,510},{8,0},{10,2},{12,4},{14,6},{16,8},... | collective-permute-start | bytes 1572872 | tf_op jit(solution)/shard_map/ppermute | solution.py:17
  133.6 12.7 %collective-permute-start = (bf16[256,1024]{1,0:T(8,128)(2,1)S(1)}, bf16[256,1024]{1,0:T(8,128)(2,1)S(1)}, u32[]{:S(2)}, u32[]{:S(2)}) collective-permute-start(bf16[256,1024]{1,0:T(8,128)(2,1)S(1)} %copy.11), channel_id=1, source_target_pairs={{0,2},{2,4},{4,6},{6,8},{8,10},{10,12},{12,14},{14,16},{16,18},{18... | collective-permute-start | bytes 1572872 | tf_op jit(solution)/shard_map/while/body/eval_jaxpr/ppermute | solution.py:17
  139.8 5.9 %collective-permute-start.1 = (f32[256]{0:T(256)S(1)}, f32[256]{0:T(256)S(1)}, u32[]{:S(2)}, u32[]{:S(2)}) collective-permute-start(f32[256]{0:T(256)S(1)} %max.25), channel_id=1, source_target_pairs={{0,2},{2,4},{4,6},{6,8},{8,10},{10,12},{12,14},{14,16},{16,18},{18... | collective-permute-start | bytes 3080 | tf_op jit(solution)/shard_map/while/body/eval_jaxpr/ppermute | solution.py:17
  142.1 4.2 %collective-permute-start.2 = (f32[256]{0:T(256)S(1)}, f32[256]{0:T(256)S(1)}, u32[]{:S(2)}, u32[]{:S(2)}) collective-permute-start(f32[256]{0:T(256)S(1)} %multiply_add_fusion.2), channel_id=1, source_target_pairs={{0,2},{2,4},{4,6},{6,8},{8,10},{10,12},{12,14},{14,16},{16,18},{18... | collective-permute-start | bytes 3080 | tf_op jit(solution)/shard_map/while/body/eval_jaxpr/ppermute | solution.py:17
  146.4 16.5 %collective-permute-start = (bf16[256,1024]{1,0:T(8,128)(2,1)S(1)}, bf16[256,1024]{1,0:T(8,128)(2,1)S(1)}, u32[]{:S(2)}, u32[]{:S(2)}) collective-permute-start(bf16[256,1024]{1,0:T(8,128)(2,1)S(1)} %copy.11), channel_id=1, source_target_pairs={{0,2},{2,4},{4,6},{6,8},{8,10},{10,12},{12,14},{14,16},{16,18},{18... | collective-permute-start | bytes 1572872 | tf_op jit(solution)/shard_map/while/body/eval_jaxpr/ppermute | solution.py:17
  153.0 7.5 %collective-permute-start.1 = (f32[256]{0:T(256)S(1)}, f32[256]{0:T(256)S(1)}, u32[]{:S(2)}, u32[]{:S(2)}) collective-permute-start(f32[256]{0:T(256)S(1)} %max.25), channel_id=1, source_target_pairs={{0,2},{2,4},{4,6},{6,8},{8,10},{10,12},{12,14},{14,16},{16,18},{18... | collective-permute-start | bytes 3080 | tf_op jit(solution)/shard_map/while/body/eval_jaxpr/ppermute | solution.py:17
  155.3 7.5 %collective-permute-start.2 = (f32[256]{0:T(256)S(1)}, f32[256]{0:T(256)S(1)}, u32[]{:S(2)}, u32[]{:S(2)}) collective-permute-start(f32[256]{0:T(256)S(1)} %multiply_add_fusion.2), channel_id=1, source_target_pairs={{0,2},{2,4},{4,6},{6,8},{8,10},{10,12},{12,14},{14,16},{16,18},{18... | collective-permute-start | bytes 3080 | tf_op jit(solution)/shard_map/while/body/eval_jaxpr/ppermute | solution.py:17
  162.9 17.6 %collective-permute-start = (bf16[256,1024]{1,0:T(8,128)(2,1)S(1)}, bf16[256,1024]{1,0:T(8,128)(2,1)S(1)}, u32[]{:S(2)}, u32[]{:S(2)}) collective-permute-start(bf16[256,1024]{1,0:T(8,128)(2,1)S(1)} %copy.11), channel_id=1, source_target_pairs={{0,2},{2,4},{4,6},{6,8},{8,10},{10,12},{12,14},{14,16},{16,18},{18... | collective-permute-start | bytes 1572872 | tf_op jit(solution)/shard_map/while/body/eval_jaxpr/ppermute | solution.py:17
  167.2 10.9 %collective-permute-start.1 = (f32[256]{0:T(256)S(1)}, f32[256]{0:T(256)S(1)}, u32[]{:S(2)}, u32[]{:S(2)}) collective-permute-start(f32[256]{0:T(256)S(1)} %max.25), channel_id=1, source_target_pairs={{0,2},{2,4},{4,6},{6,8},{8,10},{10,12},{12,14},{14,16},{16,18},{18... | collective-permute-start | bytes 3080 | tf_op jit(solution)/shard_map/while/body/eval_jaxpr/ppermute | solution.py:17
  169.6 10.9 %collective-permute-start.2 = (f32[256]{0:T(256)S(1)}, f32[256]{0:T(256)S(1)}, u32[]{:S(2)}, u32[]{:S(2)}) collective-permute-start(f32[256]{0:T(256)S(1)} %multiply_add_fusion.2), channel_id=1, source_target_pairs={{0,2},{2,4},{4,6},{6,8},{8,10},{10,12},{12,14},{14,16},{16,18},{18... | collective-permute-start | bytes 3080 | tf_op jit(solution)/shard_map/while/body/eval_jaxpr/ppermute | solution.py:17
  180.5 17.6 %collective-permute-start = (bf16[256,1024]{1,0:T(8,128)(2,1)S(1)}, bf16[256,1024]{1,0:T(8,128)(2,1)S(1)}, u32[]{:S(2)}, u32[]{:S(2)}) collective-permute-start(bf16[256,1024]{1,0:T(8,128)(2,1)S(1)} %copy.11), channel_id=1, source_target_pairs={{0,2},{2,4},{4,6},{6,8},{8,10},{10,12},{12,14},{14,16},{16,18},{18... | collective-permute-start | bytes 1572872 | tf_op jit(solution)/shard_map/while/body/eval_jaxpr/ppermute | solution.py:17
  184.9 10.9 %collective-permute-start.1 = (f32[256]{0:T(256)S(1)}, f32[256]{0:T(256)S(1)}, u32[]{:S(2)}, u32[]{:S(2)}) collective-permute-start(f32[256]{0:T(256)S(1)} %max.25), channel_id=1, source_target_pairs={{0,2},{2,4},{4,6},{6,8},{8,10},{10,12},{12,14},{14,16},{16,18},{18... | collective-permute-start | bytes 3080 | tf_op jit(solution)/shard_map/while/body/eval_jaxpr/ppermute | solution.py:17
  187.2 10.9 %collective-permute-start.2 = (f32[256]{0:T(256)S(1)}, f32[256]{0:T(256)S(1)}, u32[]{:S(2)}, u32[]{:S(2)}) collective-permute-start(f32[256]{0:T(256)S(1)} %multiply_add_fusion.2), channel_id=1, source_target_pairs={{0,2},{2,4},{4,6},{6,8},{8,10},{10,12},{12,14},{14,16},{16,18},{18... | collective-permute-start | bytes 3080 | tf_op jit(solution)/shard_map/while/body/eval_jaxpr/ppermute | solution.py:17
  198.2 17.6 %collective-permute-start = (bf16[256,1024]{1,0:T(8,128)(2,1)S(1)}, bf16[256,1024]{1,0:T(8,128)(2,1)S(1)}, u32[]{:S(2)}, u32[]{:S(2)}) collective-permute-start(bf16[256,1024]{1,0:T(8,128)(2,1)S(1)} %copy.11), channel_id=1, source_target_pairs={{0,2},{2,4},{4,6},{6,8},{8,10},{10,12},{12,14},{14,16},{16,18},{18... | collective-permute-start | bytes 1572872 | tf_op jit(solution)/shard_map/while/body/eval_jaxpr/ppermute | solution.py:17
  202.5 10.9 %collective-permute-start.1 = (f32[256]{0:T(256)S(1)}, f32[256]{0:T(256)S(1)}, u32[]{:S(2)}, u32[]{:S(2)}) collective-permute-start(f32[256]{0:T(256)S(1)} %max.25), channel_id=1, source_target_pairs={{0,2},{2,4},{4,6},{6,8},{8,10},{10,12},{12,14},{14,16},{16,18},{18... | collective-permute-start | bytes 3080 | tf_op jit(solution)/shard_map/while/body/eval_jaxpr/ppermute | solution.py:17
  204.9 10.9 %collective-permute-start.2 = (f32[256]{0:T(256)S(1)}, f32[256]{0:T(256)S(1)}, u32[]{:S(2)}, u32[]{:S(2)}) collective-permute-start(f32[256]{0:T(256)S(1)} %multiply_add_fusion.2), channel_id=1, source_target_pairs={{0,2},{2,4},{4,6},{6,8},{8,10},{10,12},{12,14},{14,16},{16,18},{18... | collective-permute-start | bytes 3080 | tf_op jit(solution)/shard_map/while/body/eval_jaxpr/ppermute | solution.py:17
  215.8 17.6 %collective-permute-start = (bf16[256,1024]{1,0:T(8,128)(2,1)S(1)}, bf16[256,1024]{1,0:T(8,128)(2,1)S(1)}, u32[]{:S(2)}, u32[]{:S(2)}) collective-permute-start(bf16[256,1024]{1,0:T(8,128)(2,1)S(1)} %copy.11), channel_id=1, source_target_pairs={{0,2},{2,4},{4,6},{6,8},{8,10},{10,12},{12,14},{14,16},{16,18},{18... | collective-permute-start | bytes 1572872 | tf_op jit(solution)/shard_map/while/body/eval_jaxpr/ppermute | solution.py:17
  220.2 10.9 %collective-permute-start.1 = (f32[256]{0:T(256)S(1)}, f32[256]{0:T(256)S(1)}, u32[]{:S(2)}, u32[]{:S(2)}) collective-permute-start(f32[256]{0:T(256)S(1)} %max.25), channel_id=1, source_target_pairs={{0,2},{2,4},{4,6},{6,8},{8,10},{10,12},{12,14},{14,16},{16,18},{18... | collective-permute-start | bytes 3080 | tf_op jit(solution)/shard_map/while/body/eval_jaxpr/ppermute | solution.py:17
  222.6 10.9 %collective-permute-start.2 = (f32[256]{0:T(256)S(1)}, f32[256]{0:T(256)S(1)}, u32[]{:S(2)}, u32[]{:S(2)}) collective-permute-start(f32[256]{0:T(256)S(1)} %multiply_add_fusion.2), channel_id=1, source_target_pairs={{0,2},{2,4},{4,6},{6,8},{8,10},{10,12},{12,14},{14,16},{16,18},{18... | collective-permute-start | bytes 3080 | tf_op jit(solution)/shard_map/while/body/eval_jaxpr/ppermute | solution.py:17
  233.5 17.6 %collective-permute-start = (bf16[256,1024]{1,0:T(8,128)(2,1)S(1)}, bf16[256,1024]{1,0:T(8,128)(2,1)S(1)}, u32[]{:S(2)}, u32[]{:S(2)}) collective-permute-start(bf16[256,1024]{1,0:T(8,128)(2,1)S(1)} %copy.11), channel_id=1, source_target_pairs={{0,2},{2,4},{4,6},{6,8},{8,10},{10,12},{12,14},{14,16},{16,18},{18... | collective-permute-start | bytes 1572872 | tf_op jit(solution)/shard_map/while/body/eval_jaxpr/ppermute | solution.py:17
  237.9 10.9 %collective-permute-start.1 = (f32[256]{0:T(256)S(1)}, f32[256]{0:T(256)S(1)}, u32[]{:S(2)}, u32[]{:S(2)}) collective-permute-start(f32[256]{0:T(256)S(1)} %max.25), channel_id=1, source_target_pairs={{0,2},{2,4},{4,6},{6,8},{8,10},{10,12},{12,14},{14,16},{16,18},{18... | collective-permute-start | bytes 3080 | tf_op jit(solution)/shard_map/while/body/eval_jaxpr/ppermute | solution.py:17
  240.2 10.9 %collective-permute-start.2 = (f32[256]{0:T(256)S(1)}, f32[256]{0:T(256)S(1)}, u32[]{:S(2)}, u32[]{:S(2)}) collective-permute-start(f32[256]{0:T(256)S(1)} %multiply_add_fusion.2), channel_id=1, source_target_pairs={{0,2},{2,4},{4,6},{6,8},{8,10},{10,12},{12,14},{14,16},{16,18},{18... | collective-permute-start | bytes 3080 | tf_op jit(solution)/shard_map/while/body/eval_jaxpr/ppermute | solution.py:17
  251.2 17.6 %collective-permute-start = (bf16[256,1024]{1,0:T(8,128)(2,1)S(1)}, bf16[256,1024]{1,0:T(8,128)(2,1)S(1)}, u32[]{:S(2)}, u32[]{:S(2)}) collective-permute-start(bf16[256,1024]{1,0:T(8,128)(2,1)S(1)} %copy.11), channel_id=1, source_target_pairs={{0,2},{2,4},{4,6},{6,8},{8,10},{10,12},{12,14},{14,16},{16,18},{18... | collective-permute-start | bytes 1572872 | tf_op jit(solution)/shard_map/while/body/eval_jaxpr/ppermute | solution.py:17
  255.5 10.9 %collective-permute-start.1 = (f32[256]{0:T(256)S(1)}, f32[256]{0:T(256)S(1)}, u32[]{:S(2)}, u32[]{:S(2)}) collective-permute-start(f32[256]{0:T(256)S(1)} %max.25), channel_id=1, source_target_pairs={{0,2},{2,4},{4,6},{6,8},{8,10},{10,12},{12,14},{14,16},{16,18},{18... | collective-permute-start | bytes 3080 | tf_op jit(solution)/shard_map/while/body/eval_jaxpr/ppermute | solution.py:17
  257.9 10.9 %collective-permute-start.2 = (f32[256]{0:T(256)S(1)}, f32[256]{0:T(256)S(1)}, u32[]{:S(2)}, u32[]{:S(2)}) collective-permute-start(f32[256]{0:T(256)S(1)} %multiply_add_fusion.2), channel_id=1, source_target_pairs={{0,2},{2,4},{4,6},{6,8},{8,10},{10,12},{12,14},{14,16},{16,18},{18... | collective-permute-start | bytes 3080 | tf_op jit(solution)/shard_map/while/body/eval_jaxpr/ppermute | solution.py:17
  268.8 13.4 %collective-permute-start.4 = (f32[256]{0:T(256)S(1)}, f32[256]{0:T(256)S(1)}, u32[]{:S(2)}, u32[]{:S(2)}) collective-permute-start(f32[256]{0:T(256)S(1)} %get-tuple-element.57), channel_id=1, source_target_pairs={{0,504},{2,506},{4,508},{6,510},{8,0},{10,2},{12,4},{14,6},{16,8},... | collective-permute-start | bytes 3080 | tf_op jit(solution)/shard_map/ppermute | solution.py:17
  279.7 9.5 %collective-permute-start.5 = (f32[256]{0:T(256)S(1)}, f32[256]{0:T(256)S(1)}, u32[]{:S(2)}, u32[]{:S(2)}) collective-permute-start(f32[256]{0:T(256)S(1)} %get-tuple-element.58), channel_id=1, source_target_pairs={{0,504},{2,506},{4,508},{6,510},{8,0},{10,2},{12,4},{14,6},{16,8},... | collective-permute-start | bytes 3080 | tf_op jit(solution)/shard_map/ppermute | solution.py:17
Sparse Core Ops, SparseCore 0:
  10.1 120.3 all-gather.5
where the time goes:
time: 308 us; the launch traced here: 304 us
  waiting for transfers between devices  153 us (50%)
  starting transfers between devices  78.9 us (26%)
  blocking collectives  29.6 us (10%)
  matrix products  19.4 us (6%)
  between operations  14.1 us (5%)
  other arithmetic  4.6 us (1%)
  local copies, waits for them, and re-layouts  3.6 us (1%)
    all_gather x1, waiting for transfers between devices, per_device(): lax.all_gather(replay_embed, 'feat', axis=1, tiled=True)  93.9 us
    ppermute x27, starting transfers between devices, shifted(): return lax.ppermute(value, axis, pairs)  78.9 us
    ppermute x27, waiting for transfers between devices, shifted(): return lax.ppermute(value, axis, pairs)  58.4 us
    dot_general x8, matrix products, fold_tile(): lax.dot_general(visitors, slab_local, (((1,), (1,)), ((), ())), preferred...  19.4 us
    all_gather x1, blocking collectives, per_device(): lax.all_gather(fresh_embed, 'feat', axis=1, tiled=True)  15.6 us
    all_gather x2, blocking collectives, merged(): pieces = jax.tree.map(lambda part: lax.all_gather(part, axis), value)  14 us
  transfers between devices with their start and end apart: 28, of which 16 were waited for; matrix products, arithmetic and copies ran while one was open for 9% of the time, Pallas kernels for 0%

commit v1 on v0

v1 whole, which is shorter than its diff:
```python
import functools
import math

import jax
import jax.numpy as jnp
from jax import lax
from jax.experimental import pallas as pl
from jax.experimental.pallas import tpu as pltpu
from jax.sharding import PartitionSpec as P

MESH = pl.DeviceIdType.MESH
WINDOW = 8
BEHIND = 3
OWN = 3
NEG_FLOOR = -1e30
LN2 = math.log(2.0)


def kernel(
    corpus,
    steps,
    scale,
    fresh_ref,
    replay_ref,
    fresh_out,
    replay_out,
    blocks,
    slab,
    scores,
    fresh_max,
    fresh_sum,
    stats,
    landed,
    local_sem,
    zf_send,
    zf_recv,
    zr_send,
    zr_recv,
    out_send,
    share_send,
    block_recv,
    stat_send,
    stat_recv,
):
    rows, half = fresh_ref.shape
    share = replay_ref.shape[0] // 2
    step_rows = share // steps
    me_c = lax.axis_index("corpus")
    me_f = lax.axis_index("feat")
    core = lax.rem(me_c, 2)
    ring = 2 * corpus
    me = me_f * corpus + me_c

    def device(offset):
        there = lax.rem(me + offset + ring, ring)
        return (lax.rem(there, corpus), there // corpus)

    def block(slot):
        return pl.ds(pl.multiple_of(slot * rows, rows), rows)

    def columns(feature_half):
        return pl.ds(pl.multiple_of(feature_half * half, half), half)

    partner = device(corpus)
    twin = device(1 - 2 * core)
    mine = columns(me_f)
    other = columns(1 - me_f)

    barrier = pltpu.get_barrier_semaphore()
    offsets = [o + p for p in (0, corpus) for o in range(-4, 5) if o + p]
    for offset in offsets:
        pl.semaphore_signal(
            barrier, inc=1, device_id=device(offset), device_id_type=MESH
        )
    pl.semaphore_wait(barrier, len(offsets))

    z_fresh = pltpu.make_async_remote_copy(
        src_ref=fresh_ref,
        dst_ref=blocks.at[block(OWN), mine],
        send_sem=zf_send,
        recv_sem=zf_recv,
        device_id=partner,
        device_id_type=MESH,
    )
    z_fresh.start()

    def z_replay(step):
        at = pl.multiple_of(step * step_rows, step_rows)
        return pltpu.make_async_remote_copy(
            src_ref=replay_ref.at[
                pl.ds(pl.multiple_of((1 - me_f) * share + at, step_rows), step_rows), :
            ],
            dst_ref=slab.at[pl.ds(at, step_rows), mine],
            send_sem=zr_send.at[step],
            recv_sem=zr_recv.at[step],
            device_id=partner,
            device_id_type=MESH,
        )

    own_fresh = pltpu.make_async_copy(
        fresh_ref, blocks.at[block(OWN), mine], local_sem.at[0]
    )
    own_replay = pltpu.make_async_copy(
        replay_ref.at[pl.ds(pl.multiple_of(me_f * share, share), share), :],
        slab.at[:, mine],
        local_sem.at[1],
    )
    own_fresh.start()
    own_replay.start()

    def spread(phase, index, source, cols, target, slot):
        return pltpu.make_async_remote_copy(
            src_ref=source,
            dst_ref=blocks.at[block(slot), cols],
            send_sem=out_send.at[phase, index],
            recv_sem=block_recv.at[phase, slot],
            device_id=target,
            device_id_type=MESH,
        )

    def outgoing(phase):
        cols = mine if phase == 0 else other
        source = fresh_ref if phase == 0 else blocks.at[block(OWN), cols]
        always = [
            spread(phase, 0, source, cols, device(-2), 5),
            spread(phase, 1, source, cols, device(2), 1),
            spread(phase, 2, source, cols, device(-4), 7),
            spread(phase, 3, source, cols, twin, 2 + 2 * core),
        ]
        return always, spread(phase, 4, source, cols, device(3), 0)

    def sharing(phase, index, slot, to):
        from_feat = device(slot - BEHIND)[1]
        cols = columns(from_feat if phase == 0 else 1 - from_feat)
        return pltpu.make_async_remote_copy(
            src_ref=blocks.at[block(slot), cols],
            dst_ref=blocks.at[block(to), cols],
            send_sem=share_send.at[phase, index],
            recv_sem=block_recv.at[phase, to],
            device_id=twin,
            device_id_type=MESH,
        )

    def arrival(phase, slot):
        pltpu.make_async_copy(
            blocks.at[block(slot), mine],
            blocks.at[block(slot), mine],
            block_recv.at[phase, slot],
        ).wait()

    def start_spread(phase):
        always, odd = outgoing(phase)
        for copy in always:
            copy.start()

        @pl.when(core == 1)
        def _():
            odd.start()

    def start_sharing(phase):
        for index, slot in enumerate((1, 5)):
            arrival(phase, slot)
            sharing(phase, index, slot, slot - 1 + 2 * core).start()
        arrival(phase, 7)

        @pl.when(core == 0)
        def _():
            sharing(phase, 2, 7, 6).start()

    def finish_spread(phase):
        always, odd = outgoing(phase)
        for copy in always:
            copy.wait_send()

        @pl.when(core == 1)
        def _():
            odd.wait_send()

        for index, slot in enumerate((1, 5)):
            sharing(phase, index, slot, slot - 1 + 2 * core).wait_send()

        @pl.when(core == 0)
        def _():
            sharing(phase, 2, 7, 6).wait_send()

    start_spread(0)
    z_fresh.wait()

    def start_replay(step, carry):
        z_replay(step).start()
        return carry

    lax.fori_loop(0, steps, start_replay, 0)
    start_spread(1)

    fresh_max[...] = jnp.full_like(fresh_max, NEG_FLOOR)
    fresh_sum[...] = jnp.zeros_like(fresh_sum)
    stats[...] = jnp.zeros_like(stats)

    for phase in (0, 1):
        start_sharing(phase)
    for phase in (0, 1):
        for slot in (0, 2, 4, 6):
            arrival(phase, slot)
    own_fresh.wait()
    own_replay.wait()

    groups = step_rows // 8
    chunk_rows = step_rows // 128

    def visit(step, carry):
        z_replay(step).wait_recv()
        at = pl.multiple_of(step * step_rows, step_rows)
        row_max = jnp.full((step_rows, 128), NEG_FLOOR, jnp.float32)
        for k in range(WINDOW):
            score = (
                lax.dot_general(
                    slab[pl.ds(at, step_rows), :],
                    blocks[k * rows : (k + 1) * rows, :],
                    (((1,), (1,)), ((), ())),
                    preferred_element_type=jnp.float32,
                )
                * scale
            )
            scores[:, k * rows : (k + 1) * rows] = score
            for j in range(rows // 128):
                row_max = jnp.maximum(row_max, score[:, j * 128 : (j + 1) * 128])
            grouped = score.reshape(groups, 8, rows)
            old = fresh_max[:, k * rows : (k + 1) * rows]
            new = jnp.maximum(old, jnp.max(grouped, axis=0))
            fresh_max[:, k * rows : (k + 1) * rows] = new
            fresh_sum[:, k * rows : (k + 1) * rows] = fresh_sum[
                :, k * rows : (k + 1) * rows
            ] * jnp.exp2(old - new) + jnp.sum(jnp.exp2(grouped - new[None]), axis=0)
        row_sum = jnp.zeros((step_rows, 128), jnp.float32)
        for j in range(WINDOW * rows // 128):
            row_sum += jnp.exp2(scores[:, j * 128 : (j + 1) * 128] - row_max)
        row_max = row_max.T
        row_sum = row_sum.T
        top = jnp.max(row_max, axis=0, keepdims=True)
        total = jnp.sum(row_sum * jnp.exp2(row_max - top), axis=0, keepdims=True)
        result = LN2 * (top + jnp.log2(total))
        for j in range(chunk_rows):
            replay_out[pl.ds(step * chunk_rows + j, 1), :] = result[
                :, j * 128 : (j + 1) * 128
            ]
        return carry

    lax.fori_loop(0, steps, visit, 0)

    for k in range(WINDOW):
        span = slice(k * rows, (k + 1) * rows)
        top = jnp.max(fresh_max[:, span], axis=0, keepdims=True)
        total = jnp.sum(
            fresh_sum[:, span] * jnp.exp2(fresh_max[:, span] - top),
            axis=0,
            keepdims=True,
        )
        for j in range(rows // 128):
            stats[k, j : j + 1, :] = top[:, j * 128 : (j + 1) * 128]
            stats[k, 2 + j : 3 + j, :] = total[:, j * 128 : (j + 1) * 128]

    def send_stats(k, side):
        return pltpu.make_async_remote_copy(
            src_ref=stats.at[k],
            dst_ref=landed.at[side, k],
            send_sem=stat_send.at[side, k],
            recv_sem=stat_recv.at[side, k],
            device_id=device(k - BEHIND + side * corpus),
            device_id_type=MESH,
        )

    outward = [
        (k, side) for side in (1, 0) for k in range(WINDOW) if side or k != BEHIND
    ]
    for k, side in outward:
        send_stats(k, side).start()
    landed[0, BEHIND] = stats[BEHIND]
    for phase in (0, 1):
        finish_spread(phase)

    def end_replay(step, carry):
        z_replay(step).wait_send()
        return carry

    lax.fori_loop(0, steps, end_replay, 0)
    for k, side in outward:
        send_stats(k, side).wait()
    got = landed[...].reshape(2 * WINDOW, 8, 128)
    top = jnp.max(got[:, 0:2, :], axis=0)
    total = jnp.sum(got[:, 2:4, :] * jnp.exp2(got[:, 0:2, :] - top[None]), axis=0)
    fresh_out[...] = LN2 * (top + jnp.log2(total))


def per_device(corpus, fresh_embed, replay_embed):
    rows, half = fresh_embed.shape
    share = replay_embed.shape[0] // 2
    steps = 4
    step_rows = share // steps
    full = 2 * half
    scale = 0.25 / math.sqrt(full) * math.log2(math.e)
    dma = pltpu.SemaphoreType.DMA
    fresh_lse, replay_lse = pl.pallas_call(
        functools.partial(kernel, corpus, steps, scale),
        out_shape=(
            jax.ShapeDtypeStruct((rows // 128, 128), jnp.float32),
            jax.ShapeDtypeStruct((share // 128, 128), jnp.float32),
        ),
        in_specs=[pl.BlockSpec(memory_space=pl.ANY)] * 2,
        out_specs=[pl.BlockSpec(memory_space=pltpu.VMEM)] * 2,
        scratch_shapes=[
            pltpu.VMEM((WINDOW * rows, full), jnp.bfloat16),
            pltpu.VMEM((share, full), jnp.bfloat16),
            pltpu.VMEM((step_rows, WINDOW * rows), jnp.float32),
            pltpu.VMEM((8, WINDOW * rows), jnp.float32),
            pltpu.VMEM((8, WINDOW * rows), jnp.float32),
            pltpu.VMEM((WINDOW, 8, 128), jnp.float32),
            pltpu.VMEM((2, WINDOW, 8, 128), jnp.float32),
            dma((2,)),
            dma,
            dma,
            dma((steps,)),
            dma((steps,)),
            dma((2, 5)),
            dma((2, 3)),
            dma((2, WINDOW)),
            dma((2, WINDOW)),
            dma((2, WINDOW)),
        ],
        compiler_params=pltpu.CompilerParams(
            collective_id=0, has_side_effects=True, vmem_limit_bytes=40 * 2**20
        ),
    )(fresh_embed, replay_embed)
    return fresh_lse.reshape(rows), replay_lse.reshape(share)


def solution(mesh):
    placed = (P("corpus", "feat"), P("corpus", "feat"))
    return jax.shard_map(
        functools.partial(per_device, mesh.shape["corpus"]),
        mesh=mesh,
        in_specs=placed,
        out_specs=(P("corpus"), P(("corpus", "feat"))),
        check_vma=False,
    )
```

time: 308 us -> 108 us (0.35)
  the two profiles are of different devices: /device:TPU:1 before, /device:TPU:119 now
where the time goes in v1:
time: 108 us
  Pallas kernels  103 us (95%)
  local copies, waits for them, and re-layouts  3.69 us (3%)
    pallas_call x1, Pallas kernels, per_device(): pl.pallas_call(functools.partial(kernel, corpus, steps, scale), out_shape...  103 us
    unnamed x6, local copies, waits for them, and re-layouts  3.69 us

profile of v1, /device:TPU:119, one launch (start us, length us, event | category | flops | bytes accessed | tf_op | source)
XLA Modules:
  0.0 107.6 jit_solution(419143054011811533)
XLA Ops:
  0.6 0.0 copy-start
  0.6 1.6 %copy-done = bf16[2048,512]{1,0:T(8,128)(2,1)S(1)} copy-done((bf16[2048,512]{1,0:T(8,128)(2,1)S(1)}, bf16[2048,512]{1,0:T(8,128)(2,1)}, u32[]{:S(2)}) %copy-start) | copy-done | bytes 2097176
  2.2 0.0 copy-start.1
  2.2 0.9 copy-done.1
  3.2 103.2 %shard_map.41 = (f32[2,128]{1,0:T(2,128)S(1)}, f32[8,128]{1,0:T(8,128)S(1)}) custom-call(bf16[256,512]{1,0:T(8,128)(2,1)S(1)} %copy-done.1, bf16[2048,512]{1,0:T(8,128)(2,1)S(1)} %copy-done), custom_call_target="tpu_custom_call" | custom-call | tf_op jit(solution)/shard_map/pallas_call | solution.py:303
  106.4 0.6 copy.6
  107.0 0.6 copy.7
Async XLA Ops:
  0.6 1.6 %copy-start = (bf16[2048,512]{1,0:T(8,128)(2,1)S(1)}, bf16[2048,512]{1,0:T(8,128)(2,1)}, u32[]{:S(2)}) copy-start(bf16[2048,512]{1,0:T(8,128)(2,1)} %replay_ref.1) | copy-start | bytes 6291460
  2.2 0.9 copy-start.1

commit v2 on v1

v2 whole, which is shorter than its diff:
```python
import functools
import math

import jax
import jax.numpy as jnp
from jax import lax
from jax.experimental import pallas as pl
from jax.experimental.pallas import tpu as pltpu
from jax.sharding import PartitionSpec as P

MESH = pl.DeviceIdType.MESH
WINDOW = 8
BEHIND = 3
OWN = 3
PLANE = 64
PIECES = 8
NEG_FLOOR = -1e30
LN2 = math.log(2.0)


def kernel(
    corpus,
    plane,
    chunks,
    first_steps,
    scale,
    fresh_ref,
    replay_ref,
    fresh_out,
    replay_out,
    blocks,
    slab,
    scores,
    fresh_max,
    fresh_sum,
    stats,
    landed,
    carried,
    local_sem,
    zf_send,
    zf_recv,
    zr_send,
    zr_recv,
    out_send,
    pass_send,
    edge_send,
    block_recv,
    swap_send,
    carry_send,
    carry_recv,
    stat_send,
    stat_recv,
):
    rows, half = fresh_ref.shape
    share = replay_ref.shape[0] // 2
    lanes = plane // PIECES
    piece = rows // PIECES
    me_c = lax.axis_index("corpus")
    me_f = lax.axis_index("feat")
    ring = 2 * corpus
    me = me_f * corpus + me_c
    here = lax.rem(me_c, plane)
    core = lax.rem(here, 2)
    column = lax.rem(here, lanes) // 2
    row = here // lanes

    def device(offset):
        there = lax.rem(me + offset + ring, ring)
        return (lax.rem(there, corpus), there // corpus)

    def block(slot):
        return pl.ds(pl.multiple_of(slot * rows, rows), rows)

    def columns(feature_half):
        return pl.ds(pl.multiple_of(feature_half * half, half), half)

    partner = device(corpus)
    twin = device(1 - 2 * core)
    mine = columns(me_f)
    other = columns(1 - me_f)
    low = here < 2
    high = here >= plane - 2
    back_source = here < 4
    ahead_source = here >= plane - 3
    carries_back = column < 2
    carries = jnp.logical_or(column != 2, core == 1)

    def carrier(p):
        there = p * lanes + 2 * column + core
        return device(there - here + jnp.where(back_source, -plane, plane))

    goal = jnp.where(
        carries_back,
        plane - 2 + core,
        jnp.where(column == 2, 0, core),
    )
    goal_slot = jnp.where(
        carries_back, jnp.where(column == 0, 5, 7), jnp.where(column == 2, 0, 1)
    )
    twice = jnp.logical_or(column == 0, jnp.logical_and(column == 3, core == 1))
    goal_two = jnp.where(column == 0, plane - 4 + core, 2)
    goal_two_slot = jnp.where(column == 0, 7, 0)
    origin = jnp.where(
        carries_back,
        plane + 2 * column + core - here,
        -lanes + 2 * column + core - here,
    )

    def signal(offset):
        pl.semaphore_signal(
            barrier, inc=1, device_id=device(offset), device_id_type=MESH
        )

    barrier = pltpu.get_barrier_semaphore()
    senders = [k + p for p in (corpus, 0) for k in range(-4, 4) if k + p]
    for offset in senders:
        signal(offset)

    @pl.when(carries)
    def _():
        signal(origin)

    def greet_carriers(place, from_column, from_core):
        def body(p, carry):
            signal(p * lanes + 2 * from_column + from_core - place)
            return carry

        lax.fori_loop(0, PIECES, body, 0)

    @pl.when(high)
    def _():
        greet_carriers(here, 0, core)
        greet_carriers(here, 1, core)

    @pl.when(low)
    def _():
        greet_carriers(here, 3, core)

    @pl.when(here == 0)
    def _():
        greet_carriers(here, 2, 1)

    @pl.when(jnp.logical_and(here >= plane - 4, here < plane - 2))
    def _():
        greet_carriers(here, 0, core)

    @pl.when(here == 2)
    def _():
        greet_carriers(here, 3, 1)

    at_seam = jnp.logical_or(low, high)
    late_last = here >= plane - 4
    is_source = jnp.logical_or(back_source, ahead_source)
    pl.semaphore_wait(
        barrier,
        len(senders)
        + jnp.where(carries, 1, 0)
        + jnp.where(twice, 1, 0)
        + jnp.where(is_source, PIECES, 0),
    )

    z_fresh = pltpu.make_async_remote_copy(
        src_ref=fresh_ref,
        dst_ref=blocks.at[block(OWN), mine],
        send_sem=zf_send,
        recv_sem=zf_recv,
        device_id=partner,
        device_id_type=MESH,
    )
    z_fresh.start()

    def z_replay(step):
        at, size = chunks[step]
        return pltpu.make_async_remote_copy(
            src_ref=replay_ref.at[
                pl.ds(pl.multiple_of((1 - me_f) * share + at, size), size), :
            ],
            dst_ref=slab.at[pl.ds(at, size), mine],
            send_sem=zr_send.at[step],
            recv_sem=zr_recv.at[step],
            device_id=partner,
            device_id_type=MESH,
        )

    own_fresh = pltpu.make_async_copy(
        fresh_ref, blocks.at[block(OWN), mine], local_sem.at[0]
    )
    own_replay = pltpu.make_async_copy(
        replay_ref.at[pl.ds(pl.multiple_of(me_f * share, share), share), :],
        slab.at[:, mine],
        local_sem.at[1],
    )

    def spread(phase):
        cols = mine if phase == 0 else other
        source = fresh_ref if phase == 0 else blocks.at[block(OWN), cols]

        def to(index, target, slot):
            return pltpu.make_async_remote_copy(
                src_ref=source,
                dst_ref=blocks.at[block(slot), cols],
                send_sem=out_send.at[phase, index],
                recv_sem=block_recv.at[phase, slot],
                device_id=target,
                device_id_type=MESH,
            )

        return [
            (jnp.logical_not(low), to(0, device(-2), 5)),
            (jnp.logical_not(high), to(1, device(2), 1)),
            (None, to(2, twin, 2 + 2 * core)),
        ]

    def edge(p):
        at = pl.ds(pl.multiple_of(p * piece, piece), piece)
        return pltpu.make_async_remote_copy(
            src_ref=fresh_ref.at[at, :],
            dst_ref=carried.at[0],
            send_sem=edge_send.at[p],
            recv_sem=carry_recv.at[0],
            device_id=carrier(p),
            device_id_type=MESH,
        )

    swap = pltpu.make_async_remote_copy(
        src_ref=carried.at[0],
        dst_ref=carried.at[1],
        send_sem=swap_send,
        recv_sem=carry_recv.at[1],
        device_id=partner,
        device_id_type=MESH,
    )

    def feature_half(phase, offset):
        sender = device(offset)[1]
        return columns(sender if phase == 0 else 1 - sender)

    def hand_over(phase):
        def to(index, target, slot):
            at = pl.ds(pl.multiple_of(slot * rows + row * piece, piece), piece)
            return pltpu.make_async_remote_copy(
                src_ref=carried.at[phase],
                dst_ref=blocks.at[at, feature_half(phase, origin)],
                send_sem=carry_send.at[phase, index],
                recv_sem=block_recv.at[phase, slot],
                device_id=device(target - here),
                device_id_type=MESH,
            )

        return [
            (carries, to(0, goal, goal_slot)),
            (twice, to(1, goal_two, goal_two_slot)),
        ]

    def passing(phase, slot):
        cols = feature_half(phase, slot - BEHIND)

        def to(index, target, there):
            return pltpu.make_async_remote_copy(
                src_ref=blocks.at[block(slot), cols],
                dst_ref=blocks.at[block(there), cols],
                send_sem=pass_send.at[phase, index],
                recv_sem=block_recv.at[phase, there],
                device_id=target,
                device_id_type=MESH,
            )

        if slot == 1:
            onward = jnp.logical_and(core == 1, jnp.logical_not(at_seam))
            return [
                (onward, to(0, device(1), 0)),
                (None, to(1, twin, 2 * core)),
            ]
        if slot == 5:
            return [
                (jnp.logical_not(at_seam), to(2, device(-2), 7)),
                (None, to(3, twin, 4 + 2 * core)),
            ]
        return [(core == 0, to(4, twin, 6))]

    def each(pairs, act):
        for condition, copy in pairs:
            if condition is None:
                act(copy)
            else:
                pl.when(condition)(functools.partial(act, copy))

    def start(copy):
        copy.start()

    def sent(copy):
        copy.wait_send()

    def arrival(phase, slot):
        pltpu.make_async_copy(
            blocks.at[block(slot), mine],
            blocks.at[block(slot), mine],
            block_recv.at[phase, slot],
        ).wait()

    def start_edge():
        @pl.when(is_source)
        def _():
            def body(p, carry):
                edge(p).start()
                return carry

            lax.fori_loop(0, PIECES, body, 0)

    def pass_on(phase, slot):
        arrival(phase, slot)
        each(passing(phase, slot), start)

    def finish_spread(phase):
        each(spread(phase), sent)
        for slot in (1, 5, 7):
            each(passing(phase, slot), sent)
        each(hand_over(phase), sent)

    def finish_edge():
        @pl.when(is_source)
        def _():
            def body(p, carry):
                edge(p).wait_send()
                return carry

            lax.fori_loop(0, PIECES, body, 0)

        @pl.when(carries)
        def _():
            swap.wait_send()

    start_edge()
    each(spread(0), start)
    own_fresh.start()
    own_replay.start()

    fresh_max[...] = jnp.full_like(fresh_max, NEG_FLOOR)
    fresh_sum[...] = jnp.zeros_like(fresh_sum)
    stats[...] = jnp.zeros_like(stats)

    @pl.when(carries)
    def _():
        pltpu.make_async_copy(carried.at[0], carried.at[0], carry_recv.at[0]).wait()
        swap.start()

    each(hand_over(0), start)
    z_fresh.wait_send()
    for step in range(len(chunks)):
        z_replay(step).start()
    for slot in (1, 5):
        pass_on(0, slot)
    z_fresh.wait_recv()
    each(spread(1), start)

    @pl.when(carries)
    def _():
        swap.wait_recv()

    each(hand_over(1), start)
    pass_on(0, 7)

    @pl.when(jnp.logical_not(at_seam))
    def _():
        for slot in (1, 5):
            pass_on(1, slot)

    @pl.when(jnp.logical_not(late_last))
    def _():
        pass_on(1, 7)

    own_fresh.wait()
    own_replay.wait()

    def score_block(at, size, slot):
        block_rows = block(slot)
        score = (
            lax.dot_general(
                slab[at : at + size, :],
                blocks[block_rows, :],
                (((1,), (1,)), ((), ())),
                preferred_element_type=jnp.float32,
            )
            * scale
        )
        scores[slot, :size, :] = score
        grouped = score.reshape(size // 8, 8, rows)
        old = fresh_max[slot]
        new = jnp.maximum(old, jnp.max(grouped, axis=0))
        fresh_max[slot] = new
        fresh_sum[slot] = fresh_sum[slot] * jnp.exp2(old - new) + jnp.sum(
            jnp.exp2(grouped - new[None]), axis=0
        )

    def finish_rows(at, start_row, size):
        tiles = [
            scores[k, start_row : start_row + size, j : j + 128]
            for k in range(WINDOW)
            for j in range(0, rows, 128)
        ]
        row_max = functools.reduce(jnp.maximum, tiles)
        row_sum = functools.reduce(
            jnp.add, [jnp.exp2(tile - row_max) for tile in tiles]
        )
        row_max = row_max.T
        row_sum = row_sum.T
        top = jnp.max(row_max, axis=0, keepdims=True)
        total = jnp.sum(row_sum * jnp.exp2(row_max - top), axis=0, keepdims=True)
        first = at // 128
        replay_out[first : first + 1, :] = LN2 * (top + jnp.log2(total))

    first_rows = sum(size for _, size in chunks[:first_steps])
    for step in range(first_steps):
        z_replay(step).wait_recv()

    def visit_block(index, carry):
        slot = jnp.where(here < plane // 2, WINDOW - 1 - index, index)

        @pl.when(lax.rem(slot, 2) == 0)
        def _():
            for phase in (0, 1):
                arrival(phase, slot)

        for late, there in ((at_seam, 1), (at_seam, 5), (late_last, 7)):

            @pl.when(jnp.logical_and(late, slot == there))
            def _(there=there):
                pass_on(1, there)

        score_block(0, first_rows, slot)
        return carry

    lax.fori_loop(0, WINDOW, visit_block, 0)
    for at in range(0, first_rows, 128):
        finish_rows(at, at, 128)

    for step in range(first_steps, len(chunks)):
        at, size = chunks[step]
        z_replay(step).wait_recv()
        for slot in range(WINDOW):
            score_block(at, size, slot)
        for start_row in range(0, size, 128):
            finish_rows(at + start_row, start_row, 128)

    for k in range(WINDOW):
        top = jnp.max(fresh_max[k], axis=0, keepdims=True)
        total = jnp.sum(
            fresh_sum[k] * jnp.exp2(fresh_max[k] - top), axis=0, keepdims=True
        )
        for j in range(rows // 128):
            stats[k, j : j + 1, :] = top[:, j * 128 : (j + 1) * 128]
            stats[k, 2 + j : 3 + j, :] = total[:, j * 128 : (j + 1) * 128]

    def send_stats(k, side):
        return pltpu.make_async_remote_copy(
            src_ref=stats.at[k],
            dst_ref=landed.at[side, k],
            send_sem=stat_send.at[side, k],
            recv_sem=stat_recv.at[side, k],
            device_id=device(k - BEHIND + side * corpus),
            device_id_type=MESH,
        )

    outward = [
        (k, side) for side in (1, 0) for k in range(WINDOW) if side or k != BEHIND
    ]
    for k, side in outward:
        send_stats(k, side).start()
    landed[0, BEHIND] = stats[BEHIND]
    finish_edge()
    for phase in (0, 1):
        finish_spread(phase)
    for step in range(len(chunks)):
        z_replay(step).wait_send()
    for k, side in outward:
        send_stats(k, side).wait()
    got = landed[...].reshape(2 * WINDOW, 8, 128)
    top = jnp.max(got[:, 0:2, :], axis=0)
    total = jnp.sum(got[:, 2:4, :] * jnp.exp2(got[:, 0:2, :] - top[None]), axis=0)
    fresh_out[...] = LN2 * (top + jnp.log2(total))


def per_device(corpus, plane, fresh_embed, replay_embed):
    rows, half = fresh_embed.shape
    share = replay_embed.shape[0] // 2
    sizes = (128, 128, 256, 256, 128, 128)
    chunks = [(sum(sizes[:i]), size) for i, size in enumerate(sizes)]
    first_steps = 3
    most = max(sum(sizes[:first_steps]), max(sizes))
    full = 2 * half
    scale = 0.25 / math.sqrt(full) * math.log2(math.e)
    dma = pltpu.SemaphoreType.DMA
    fresh_lse, replay_lse = pl.pallas_call(
        functools.partial(kernel, corpus, plane, chunks, first_steps, scale),
        out_shape=(
            jax.ShapeDtypeStruct((rows // 128, 128), jnp.float32),
            jax.ShapeDtypeStruct((share // 128, 128), jnp.float32),
        ),
        in_specs=[pl.BlockSpec(memory_space=pltpu.HBM)] * 2,
        out_specs=[pl.BlockSpec(memory_space=pltpu.VMEM)] * 2,
        scratch_shapes=[
            pltpu.VMEM((WINDOW * rows, full), jnp.bfloat16),
            pltpu.VMEM((share, full), jnp.bfloat16),
            pltpu.VMEM((WINDOW, most, rows), jnp.float32),
            pltpu.VMEM((WINDOW, 8, rows), jnp.float32),
            pltpu.VMEM((WINDOW, 8, rows), jnp.float32),
            pltpu.VMEM((WINDOW, 8, 128), jnp.float32),
            pltpu.VMEM((2, WINDOW, 8, 128), jnp.float32),
            pltpu.VMEM((2, rows // PIECES, half), jnp.bfloat16),
            dma((2,)),
            dma,
            dma,
            dma((len(chunks),)),
            dma((len(chunks),)),
            dma((2, 3)),
            dma((2, 5)),
            dma((PIECES,)),
            dma((2, WINDOW)),
            dma,
            dma((2, 2)),
            dma((2,)),
            dma((2, WINDOW)),
            dma((2, WINDOW)),
        ],
        compiler_params=pltpu.CompilerParams(
            collective_id=0, has_side_effects=True, vmem_limit_bytes=60 * 2**20
        ),
    )(fresh_embed, replay_embed)
    return fresh_lse.reshape(rows), replay_lse.reshape(share)


def solution(mesh):
    placed = (P("corpus", "feat"), P("corpus", "feat"))
    return jax.shard_map(
        functools.partial(per_device, mesh.shape["corpus"], PLANE),
        mesh=mesh,
        in_specs=placed,
        out_specs=(P("corpus"), P(("corpus", "feat"))),
        check_vma=False,
    )
```

time: 108 us -> 97.3 us (0.901)
  the two profiles are of different devices: /device:TPU:119 before, /device:TPU:65 now
where the time goes in v2:
time: 97.3 us; the launch traced here: 97.1 us
  Pallas kernels  94 us (97%)
  local copies, waits for them, and re-layouts  2.48 us (3%)
    pallas_call x1, Pallas kernels, per_device(): pl.pallas_call(functools.partial(kernel, corpus, plane, chunks, first_ste...  94 us
    unnamed x2, local copies, waits for them, and re-layouts  2.48 us

profile of v2, /device:TPU:65, one launch (start us, length us, event | category | flops | bytes accessed | tf_op | source)
XLA Modules:
  0.0 97.1 jit_solution(12706518625036584629)
XLA Ops:
  0.6 94.0 %shard_map.41 = (f32[2,128]{1,0:T(2,128)}, f32[8,128]{1,0:T(8,128)}) custom-call(bf16[256,512]{1,0:T(8,128)(2,1)} %fresh_ref.1, bf16[2048,512]{1,0:T(8,128)(2,1)} %replay_ref.1), custom_call_target="tpu_custom_call" | custom-call | tf_op jit(solution)/shard_map/pallas_call | solution.py:493
  94.7 1.2 %copy.6 = f32[256]{0:T(256)} copy(f32[256]{0:T(256)} %bitcast.3) | data formatting | bytes 2048
  95.9 1.3 %copy.7 = f32[1024]{0:T(1024)} copy(f32[1024]{0:T(1024)} %bitcast.2) | data formatting | bytes 8192

commit v3 on v2

--- a/solution.py
+++ b/solution.py
@@ -16,6 +16,7 @@
 PIECES = 8
 NEG_FLOOR = -1e30
 LN2 = math.log(2.0)
+PARTS = 2
 
 
 def kernel(
@@ -68,8 +69,12 @@
         there = lax.rem(me + offset + ring, ring)
         return (lax.rem(there, corpus), there // corpus)
 
-    def block(slot):
-        return pl.ds(pl.multiple_of(slot * rows, rows), rows)
+    sub = rows // PARTS
+
+    def block(slot, part=0):
+        if part == 0:
+            return pl.ds(pl.multiple_of(slot * rows, rows), rows)
+        return pl.ds(pl.multiple_of(slot * rows + (part - 1) * sub, sub), sub)
 
     def columns(feature_half):
         return pl.ds(pl.multiple_of(feature_half * half, half), half)
@@ -149,7 +154,6 @@
         greet_carriers(here, 3, 1)
 
     at_seam = jnp.logical_or(low, high)
-    late_last = here >= plane - 4
     is_source = jnp.logical_or(back_source, ahead_source)
     pl.semaphore_wait(
         barrier,
@@ -159,15 +163,18 @@
         + jnp.where(is_source, PIECES, 0),
     )
 
-    z_fresh = pltpu.make_async_remote_copy(
-        src_ref=fresh_ref,
-        dst_ref=blocks.at[block(OWN), mine],
-        send_sem=zf_send,
-        recv_sem=zf_recv,
-        device_id=partner,
-        device_id_type=MESH,
-    )
-    z_fresh.start()
+    def z_fresh(part):
+        return pltpu.make_async_remote_copy(
+            src_ref=fresh_ref.at[pl.ds((part - 1) * sub, sub), :],
+            dst_ref=blocks.at[block(OWN, part), mine],
+            send_sem=zf_send.at[part - 1],
+            recv_sem=zf_recv.at[part - 1],
+            device_id=partner,
+            device_id_type=MESH,
+        )
+
+    for part in range(1, PARTS + 1):
+        z_fresh(part).start()
 
     def z_replay(step):
         at, size = chunks[step]
@@ -191,16 +198,16 @@
         local_sem.at[1],
     )
 
-    def spread(phase):
-        cols = mine if phase == 0 else other
-        source = fresh_ref if phase == 0 else blocks.at[block(OWN), cols]
+    def spread(part):
+        cols = mine if part == 0 else other
+        source = fresh_ref if part == 0 else blocks.at[block(OWN, part), cols]
 
         def to(index, target, slot):
             return pltpu.make_async_remote_copy(
                 src_ref=source,
-                dst_ref=blocks.at[block(slot), cols],
-                send_sem=out_send.at[phase, index],
-                recv_sem=block_recv.at[phase, slot],
+                dst_ref=blocks.at[block(slot, part), cols],
+                send_sem=out_send.at[part, index],
+                recv_sem=block_recv.at[part, slot],
                 device_id=target,
                 device_id_type=MESH,
             )
@@ -242,7 +249,9 @@
                 src_ref=carried.at[phase],
                 dst_ref=blocks.at[at, feature_half(phase, origin)],
                 send_sem=carry_send.at[phase, index],
-                recv_sem=block_recv.at[phase, slot],
+                recv_sem=block_recv.at[
+                    0 if phase == 0 else 1 + row * PARTS // PIECES, slot
+                ],
                 device_id=device(target - here),
                 device_id_type=MESH,
             )
@@ -252,15 +261,15 @@
             (twice, to(1, goal_two, goal_two_slot)),
         ]
 
-    def passing(phase, slot):
-        cols = feature_half(phase, slot - BEHIND)
+    def passing(part, slot):
+        cols = feature_half(min(part, 1), slot - BEHIND)
 
         def to(index, target, there):
             return pltpu.make_async_remote_copy(
-                src_ref=blocks.at[block(slot), cols],
-                dst_ref=blocks.at[block(there), cols],
-                send_sem=pass_send.at[phase, index],
-                recv_sem=block_recv.at[phase, there],
+                src_ref=blocks.at[block(slot, part), cols],
+                dst_ref=blocks.at[block(there, part), cols],
+                send_sem=pass_send.at[part, index],
+                recv_sem=block_recv.at[part, there],
                 device_id=target,
                 device_id_type=MESH,
             )
@@ -291,11 +300,11 @@
     def sent(copy):
         copy.wait_send()
 
-    def arrival(phase, slot):
+    def arrival(part, slot):
         pltpu.make_async_copy(
-            blocks.at[block(slot), mine],
-            blocks.at[block(slot), mine],
-            block_recv.at[phase, slot],
+            blocks.at[block(slot, part), mine],
+            blocks.at[block(slot, part), mine],
+            block_recv.at[part, slot],
         ).wait()
 
     def start_edge():
@@ -307,15 +316,11 @@
 
             lax.fori_loop(0, PIECES, body, 0)
 
-    def pass_on(phase, slot):
-        arrival(phase, slot)
-        each(passing(phase, slot), start)
-
-    def finish_spread(phase):
-        each(spread(phase), sent)
-        for slot in (1, 5, 7):
-            each(passing(phase, slot), sent)
-        each(hand_over(phase), sent)
+    def pass_on(part, slot):
+        arrival(part, slot)
+        each(passing(part, slot), start)
+
+    later = range(1, PARTS + 1)
 
     def finish_edge():
         @pl.when(is_source)
@@ -345,13 +350,16 @@
         swap.start()
 
     each(hand_over(0), start)
-    z_fresh.wait_send()
-    for step in range(len(chunks)):
-        z_replay(step).start()
+    for part in later:
+        z_fresh(part).wait_send()
+    z_replay(0).start()
     for slot in (1, 5):
         pass_on(0, slot)
-    z_fresh.wait_recv()
-    each(spread(1), start)
+    for part in later:
+        z_fresh(part).wait_recv()
+        each(spread(part), start)
+    for step in range(1, len(chunks)):
+        z_replay(step).start()
 
     @pl.when(carries)
     def _():
@@ -360,14 +368,11 @@
     each(hand_over(1), start)
     pass_on(0, 7)
 
-    @pl.when(jnp.logical_not(at_seam))
-    def _():
+    for part in later:
         for slot in (1, 5):
-            pass_on(1, slot)
-
-    @pl.when(jnp.logical_not(late_last))
-    def _():
-        pass_on(1, 7)
+            pass_on(part, slot)
+    for part in later:
+        pass_on(part, 7)
 
     own_fresh.wait()
     own_replay.wait()
@@ -418,14 +423,8 @@
 
         @pl.when(lax.rem(slot, 2) == 0)
         def _():
-            for phase in (0, 1):
-                arrival(phase, slot)
-
-        for late, there in ((at_seam, 1), (at_seam, 5), (late_last, 7)):
-
-            @pl.when(jnp.logical_and(late, slot == there))
-            def _(there=there):
-                pass_on(1, there)
+            for part in range(PARTS + 1):
+                arrival(part, slot)
 
         score_block(0, first_rows, slot)
         return carry
@@ -469,7 +468,11 @@
     landed[0, BEHIND] = stats[BEHIND]
     finish_edge()
     for phase in (0, 1):
-        finish_spread(phase)
+        each(hand_over(phase), sent)
+    for part in range(PARTS + 1):
+        each(spread(part), sent)
+        for slot in (1, 5, 7):
+            each(passing(part, slot), sent)
     for step in range(len(chunks)):
         z_replay(step).wait_send()
     for k, side in outward:
@@ -508,14 +511,14 @@
             pltpu.VMEM((2, WINDOW, 8, 128), jnp.float32),
             pltpu.VMEM((2, rows // PIECES, half), jnp.bfloat16),
             dma((2,)),
-            dma,
-            dma,
+            dma((PARTS,)),
+            dma((PARTS,)),
             dma((len(chunks),)),
             dma((len(chunks),)),
-            dma((2, 3)),
-            dma((2, 5)),
+            dma((PARTS + 1, 3)),
+            dma((PARTS + 1, 5)),
             dma((PIECES,)),
-            dma((2, WINDOW)),
+            dma((PARTS + 1, WINDOW)),
             dma,
             dma((2, 2)),
             dma((2,)),

time: 97.3 us -> 94.4 us (0.970)
  the two profiles are of different devices: /device:TPU:65 before, /device:TPU:1 now
where the time goes in v3:
time: 94.4 us; the launch traced here: 94.2 us
  Pallas kernels  91.1 us (97%)
  local copies, waits for them, and re-layouts  2.48 us (3%)
    pallas_call x1, Pallas kernels, per_device(): pl.pallas_call(functools.partial(kernel, corpus, plane, chunks, first_ste...  91.1 us
    unnamed x2, local copies, waits for them, and re-layouts  2.48 us

profile of v3, /device:TPU:1, one launch (start us, length us, event | category | flops | bytes accessed | tf_op | source)
XLA Modules:
  0.0 94.2 jit_solution(2451665361491493907)
XLA Ops:
  0.6 91.1 %shard_map.41 = (f32[2,128]{1,0:T(2,128)}, f32[8,128]{1,0:T(8,128)}) custom-call(bf16[256,512]{1,0:T(8,128)(2,1)} %fresh_ref.1, bf16[2048,512]{1,0:T(8,128)(2,1)} %replay_ref.1), custom_call_target="tpu_custom_call" | custom-call | tf_op jit(solution)/shard_map/pallas_call | solution.py:496
  91.8 1.2 %copy.6 = f32[256]{0:T(256)} copy(f32[256]{0:T(256)} %bitcast.3) | data formatting | bytes 2048
  93.0 1.3 %copy.7 = f32[1024]{0:T(1024)} copy(f32[1024]{0:T(1024)} %bitcast.2) | data formatting | bytes 8192

commit v4 on v3

--- a/solution.py
+++ b/solution.py
@@ -16,6 +16,7 @@
 PIECES = 8
 NEG_FLOOR = -1e30
 LN2 = math.log(2.0)
+VMEM_BYTES = 55104 * 1024
 PARTS = 2
 
 
@@ -117,7 +118,7 @@
         )
 
     barrier = pltpu.get_barrier_semaphore()
-    senders = [k + p for p in (corpus, 0) for k in range(-4, 4) if k + p]
+    senders = [corpus] + [k + p for p in (corpus, 0) for k in range(-4, 4) if k]
     for offset in senders:
         signal(offset)
 
@@ -173,8 +174,6 @@
             device_id_type=MESH,
         )
 
-    for part in range(1, PARTS + 1):
-        z_fresh(part).start()
 
     def z_replay(step):
         at, size = chunks[step]
@@ -335,7 +334,10 @@
         def _():
             swap.wait_send()
 
+    z_fresh(1).start()
     start_edge()
+    for part in later[1:]:
+        z_fresh(part).start()
     each(spread(0), start)
     own_fresh.start()
     own_replay.start()
@@ -438,8 +440,9 @@
         z_replay(step).wait_recv()
         for slot in range(WINDOW):
             score_block(at, size, slot)
-        for start_row in range(0, size, 128):
-            finish_rows(at + start_row, start_row, 128)
+        if step < len(chunks) - 1:
+            for start_row in range(0, size, 128):
+                finish_rows(at + start_row, start_row, 128)
 
     for k in range(WINDOW):
         top = jnp.max(fresh_max[k], axis=0, keepdims=True)
@@ -466,6 +469,9 @@
     for k, side in outward:
         send_stats(k, side).start()
     landed[0, BEHIND] = stats[BEHIND]
+    at, size = chunks[-1]
+    for start_row in range(0, size, 128):
+        finish_rows(at + start_row, start_row, 128)
     finish_edge()
     for phase in (0, 1):
         each(hand_over(phase), sent)
@@ -526,7 +532,7 @@
             dma((2, WINDOW)),
         ],
         compiler_params=pltpu.CompilerParams(
-            collective_id=0, has_side_effects=True, vmem_limit_bytes=60 * 2**20
+            collective_id=0, has_side_effects=True, vmem_limit_bytes=VMEM_BYTES
         ),
     )(fresh_embed, replay_embed)
     return fresh_lse.reshape(rows), replay_lse.reshape(share)

time: 94.4 us -> 92.1 us (0.976)
  local copies, waits for them, and re-layouts: 2.48 us -> 1.16 us
    unnamed x2, local copies, waits for them, and re-layouts: 2.48 us -> 1.16 us
where the time goes in v4:
time: 92.1 us; the launch traced here: 92 us
  Pallas kernels  90.2 us (98%)
  local copies, waits for them, and re-layouts  1.16 us (1%)
    pallas_call x1, Pallas kernels, per_device(): pl.pallas_call(functools.partial(kernel, corpus, plane, chunks, first_ste...  90.2 us

profile of v4, /device:TPU:1, one launch (start us, length us, event | category | flops | bytes accessed | tf_op | source)
XLA Modules:
  0.0 92.0 jit_solution(1873527988634834720)
XLA Ops:
  0.6 90.2 %shard_map.41 = (f32[2,128]{1,0:T(2,128)S(1)}, f32[8,128]{1,0:T(8,128)S(1)}) custom-call(bf16[256,512]{1,0:T(8,128)(2,1)} %fresh_ref.1, bf16[2048,512]{1,0:T(8,128)(2,1)} %replay_ref.1), custom_call_target="tpu_custom_call" | custom-call | tf_op jit(solution)/shard_map/pallas_call | solution.py:502
  90.9 0.6 copy.6
  91.4 0.6 copy.7

commit v5 on v4

--- a/solution.py
+++ b/solution.py
@@ -492,9 +492,9 @@
 def per_device(corpus, plane, fresh_embed, replay_embed):
     rows, half = fresh_embed.shape
     share = replay_embed.shape[0] // 2
-    sizes = (128, 128, 256, 256, 128, 128)
+    sizes = (256, 256, 256, 128, 128)
     chunks = [(sum(sizes[:i]), size) for i, size in enumerate(sizes)]
-    first_steps = 3
+    first_steps = 2
     most = max(sum(sizes[:first_steps]), max(sizes))
     full = 2 * half
     scale = 0.25 / math.sqrt(full) * math.log2(math.e)

time: 92.1 us -> 89.8 us (0.975)
  the two profiles are of different devices: /device:TPU:1 before, /device:TPU:137 now
where the time goes in v5:
time: 89.8 us; the launch traced here: 89.7 us
  Pallas kernels  87.9 us (98%)
  local copies, waits for them, and re-layouts  1.16 us (1%)
    pallas_call x1, Pallas kernels, per_device(): pl.pallas_call(functools.partial(kernel, corpus, plane, chunks, first_ste...  87.9 us

profile of v5, /device:TPU:137, one launch (start us, length us, event | category | flops | bytes accessed | tf_op | source)
XLA Modules:
  0.0 89.7 jit_solution(3088119067895994714)
XLA Ops:
  0.6 87.9 %shard_map.41 = (f32[2,128]{1,0:T(2,128)S(1)}, f32[8,128]{1,0:T(8,128)S(1)}) custom-call(bf16[256,512]{1,0:T(8,128)(2,1)} %fresh_ref.1, bf16[2048,512]{1,0:T(8,128)(2,1)} %replay_ref.1), custom_call_target="tpu_custom_call" | custom-call | tf_op jit(solution)/shard_map/pallas_call | solution.py:502
  88.6 0.6 copy.6
  89.1 0.6 copy.7

commit v6 on v5

--- a/solution.py
+++ b/solution.py
@@ -354,13 +354,14 @@
     each(hand_over(0), start)
     for part in later:
         z_fresh(part).wait_send()
-    z_replay(0).start()
+    for step in range(2):
+        z_replay(step).start()
     for slot in (1, 5):
         pass_on(0, slot)
     for part in later:
         z_fresh(part).wait_recv()
         each(spread(part), start)
-    for step in range(1, len(chunks)):
+    for step in range(2, len(chunks)):
         z_replay(step).start()
 
     @pl.when(carries)

time: 89.8 us -> 89.9 us (level)
  the two profiles are of different devices: /device:TPU:137 before, /device:TPU:1 now
where the time goes in v6:
time: 89.9 us; the launch traced here: 88.4 us
  Pallas kernels  86.6 us (96%)
  local copies, waits for them, and re-layouts  1.16 us (1%)
    pallas_call x1, Pallas kernels, per_device(): pl.pallas_call(functools.partial(kernel, corpus, plane, chunks, first_ste...  86.6 us

profile of v6, /device:TPU:1, one launch (start us, length us, event | category | flops | bytes accessed | tf_op | source)
XLA Modules:
  0.0 88.4 jit_solution(185171868690853314)
XLA Ops:
  0.6 86.6 %shard_map.41 = (f32[2,128]{1,0:T(2,128)S(1)}, f32[8,128]{1,0:T(8,128)S(1)}) custom-call(bf16[256,512]{1,0:T(8,128)(2,1)} %fresh_ref.1, bf16[2048,512]{1,0:T(8,128)(2,1)} %replay_ref.1), custom_call_target="tpu_custom_call" | custom-call | tf_op jit(solution)/shard_map/pallas_call | solution.py:503
  87.3 0.6 copy.6
  87.8 0.6 copy.7
